TPU v7x, 256 devices: a whole 4x4x8 slice. The times are simulated.
256 devices in a mesh: dp: 16 (over z, x_lo), tensor: 16 (over y, x_hi, core).
Axes of the slice: x: 4 (x_hi: 2, x_lo: 2; x = x_hi * 2 + x_lo), y: 4, z: 8, core: 2. Of those that a mesh axis runs over, the one named last changes fastest.
Arguments:
- gate_pre: bfloat16 [4096, 18432], P('dp', 'tensor'), may hold values from -6 to 6
- up_pre: bfloat16 [4096, 18432], P('dp', 'tensor'), may hold values from -6 to 6
- down_weight: bfloat16 [18432, 4608], P('tensor'), may hold values from -0.046875 to 0.046875
- out_grad: bfloat16 [4096, 4608], P(('dp', 'tensor')), may hold values from -24 to 24
Outputs:
- layer_out: bfloat16 [4096, 4608], P(('dp', 'tensor'))
- grad_gate: bfloat16 [4096, 18432], P('dp', 'tensor')
- grad_up: bfloat16 [4096, 18432], P('dp', 'tensor')
- grad_down: bfloat16 [18432, 4608], P('tensor', 'dp')
All inputs are finite; a program needn't handle non-finite values.
Results may differ from a plain program's by a relative error of at most 0.023.
Values may be sent and summed in bfloat16 or wider, within the bound.
A program may use at most 128 MiB of HBM per device.

v0:
```python
import math

import jax
import jax.numpy as jnp
from jax import lax
from jax.sharding import PartitionSpec as P


def gelu_and_slope(value):
    coeff = math.sqrt(2.0 / math.pi)
    inner = coeff * (value + 0.044715 * value * value * value)
    tangent = jnp.tanh(inner)
    gelu = 0.5 * value * (1.0 + tangent)
    slope = 0.5 * (1.0 + tangent) + 0.5 * value * (1.0 - tangent * tangent) * coeff * (
        1.0 + 3.0 * 0.044715 * value * value
    )
    return (gelu, slope)


def body(gate_pre, up_pre, down_weight, out_grad):
    gate_value = gate_pre.astype(jnp.float32)
    up_value = up_pre.astype(jnp.float32)
    gelu, slope = gelu_and_slope(gate_value)
    hidden = (gelu * up_value).astype(jnp.bfloat16)
    layer_out = lax.psum_scatter(
        jnp.dot(hidden, down_weight, preferred_element_type=jnp.float32).astype(jnp.bfloat16),
        "tensor",
        scatter_dimension=0,
        tiled=True,
    )
    group_grad = lax.all_gather(out_grad, "tensor", axis=0, tiled=True)
    grad_hidden = lax.dot_general(
        group_grad, down_weight, (((1,), (1,)), ((), ())), preferred_element_type=jnp.float32
    )
    grad_gate = (grad_hidden * up_value * slope).astype(jnp.bfloat16)
    grad_up = (grad_hidden * gelu).astype(jnp.bfloat16)
    summed = lax.psum_scatter(
        lax.dot_general(
            group_grad, hidden, (((0,), (0,)), ((), ())), preferred_element_type=jnp.float32
        ).astype(jnp.bfloat16),
        "dp",
        scatter_dimension=0,
        tiled=True,
    ).astype(jnp.float32)
    grad_down = summed.T.astype(jnp.bfloat16)
    return (layer_out, grad_gate, grad_up, grad_down)


def solution(mesh):
    return jax.shard_map(
        body,
        mesh=mesh,
        in_specs=(
            P("dp", "tensor"),
            P("dp", "tensor"),
            P("tensor", None),
            P(("dp", "tensor"), None),
        ),
        out_specs=(
            P(("dp", "tensor"), None),
            P("dp", "tensor"),
            P("dp", "tensor"),
            P("tensor", "dp"),
        ),
        check_vma=False,
    )
```

profile of v0, /device:TPU:16, one launch (start us, length us, event | category | flops | bytes accessed | tf_op | source)
XLA Modules:
  0.0 387.2 jit_solution(570142984614019498)
XLA Ops:
  7.2 0.0 all-gather.2.cloned.1.call-start
  7.2 0.7 all-gather.2.cloned.1.call-update
  7.9 0.0 reduce-scatter.5.cloned.1.call-start
  7.9 9.2 %convolution_convert_fusion.1 = bf16[256,4608]{1,0:T(8,128)(2,1)} fusion(bf16[1152,4608]{1,0:T(8,128)(2,1)} %param.6, bf16[256,1152]{1,0:T(8,128)(2,1)} %param.5, bf16[256,1152]{1,0:T(8,128)(2,1)} %param.4), kind=kOutput, calls=%fused_computation.2 | convolution fusion | flops 2722627584 | bytes 14155776 | tf_op jit(solution)/shard_map/dot_general | solution.py:26
  17.2 0.0 copy-start.1
  17.2 0.0 copy-start.2
  17.2 0.0 reduce-scatter.5.cloned.1.call-update
  17.2 0.0 reduce-scatter.7.cloned.1.call-start
  17.3 48.2 %all-gather.2.cloned.1.call-done = bf16[256,4608]{1,0:T(8,128)(2,1)} async-done(((bf16[16,4608]{1,0:T(8,128)(2,1)}), bf16[256,4608]{1,0:T(8,128)(2,1)}) %all-gather.2.cloned.1.call-update) | async-done | bytes 2359312 | tf_op jit(solution)/shard_map/all_gather | solution.py:31
  65.4 0.0 copy-done.1
  65.4 0.0 copy-done.2
  65.4 8.9 %fusion = bf16[4608,1152]{0,1:T(8,128)(2,1)} fusion(bf16[256,4608]{1,0:T(8,128)(2,1)} %all-gather.2.cloned.1.call-done, bf16[256,1152]{1,0:T(8,128)(2,1)S(1)} %copy-done.1, bf16[256,1152]{1,0:T(8,128)(2,1)S(1)} %copy-done.2), kind=kOutput, calls=%fused_computation.1 | convolution fusion | flops 2726756352 | bytes 14155776 | tf_op jit(solution)/shard_map/dot_general | solution.py:38
  74.3 15.2 %copy.10 = bf16[4608,1152]{1,0:T(8,128)(2,1)} copy(bf16[4608,1152]{0,1:T(8,128)(2,1)} %fusion) | data formatting | bytes 21233664
  89.6 0.0 copy-start
  89.6 0.0 reduce-scatter.7.cloned.1.call-update
  89.6 1.7 copy-done
  91.3 9.1 %multiply_convert_fusion = (bf16[256,1152]{1,0:T(8,128)(2,1)}, bf16[256,1152]{1,0:T(8,128)(2,1)}) fusion(bf16[256,1152]{1,0:T(8,128)(2,1)S(1)} %copy-done.2, bf16[256,1152]{1,0:T(8,128)(2,1)S(1)} %copy-done.1, bf16[256,4608]{1,0:T(8,128)(2,1)S(1)} %copy-done, bf16[1152,4608]{1,0:T(8,128)(2,1)} %param.6), kind=kOutput, calls=%fused_computation.23 | convolution fusion | flops 2725281792 | bytes 15335424 | tf_op jit(solution)/shard_map/dot_general | solution.py:32
  100.4 48.8 %reduce-scatter.5.cloned.1.call-done = bf16[16,4608]{1,0:T(8,128)(2,1)} async-done(((bf16[256,4608]{1,0:T(8,128)(2,1)}), bf16[16,4608]{1,0:T(8,128)(2,1)}) %reduce-scatter.5.cloned.1.call-update) | async-done | bytes 147472 | tf_op jit(solution)/shard_map/reduce_scatter | solution.py:25
  149.1 231.5 %reduce-scatter.7.cloned.1.call-done = bf16[288,1152]{1,0:T(8,128)(2,1)} async-done(((bf16[4608,1152]{1,0:T(8,128)(2,1)}), bf16[288,1152]{1,0:T(8,128)(2,1)}) %reduce-scatter.7.cloned.1.call-update) | async-done | bytes 663568
Async XLA Ops:
  7.2 58.3 %all-gather.2.cloned.1.call-start = ((), (), s32[]{:S(2)}) async-start(), calls=%async_computation.3 | async-start | bytes 2506752 | tf_op jit(solution)/shard_map/all_gather | solution.py:31
  7.9 141.2 %reduce-scatter.5.cloned.1.call-start = ((), (), s32[]{:S(2)}) async-start(), calls=%async_computation.2 | async-start | bytes 2506752 | tf_op jit(solution)/shard_map/reduce_scatter | solution.py:25
  17.2 48.3 %copy-start.1 = (bf16[256,1152]{1,0:T(8,128)(2,1)S(1)}, bf16[256,1152]{1,0:T(8,128)(2,1)}, u32[]{:S(2)}) copy-start(bf16[256,1152]{1,0:T(8,128)(2,1)} %param.5) | copy-start | bytes 1769476
  17.2 48.3 %copy-start.2 = (bf16[256,1152]{1,0:T(8,128)(2,1)S(1)}, bf16[256,1152]{1,0:T(8,128)(2,1)}, u32[]{:S(2)}) copy-start(bf16[256,1152]{1,0:T(8,128)(2,1)} %param.4) | copy-start | bytes 1769476
  17.2 363.4 %reduce-scatter.7.cloned.1.call-start = ((), (), s32[]{:S(2)}) async-start(), calls=%async_computation.4 | async-start | bytes 11280384
  89.6 1.7 copy-start
Sparse Core Ops, SparseCore 0:
  10.8 54.6 all-gather.1
  70.3 78.7 reduce-scatter.4
  152.4 228.1 reduce-scatter.6
where the time goes:
time: 389 us; the launch traced here: 387 us
  waiting for transfers between devices  329 us (85%)
  matrix products  27.2 us (7%)
  local copies, waits for them, and re-layouts  17 us (4%)
  between operations  13.7 us (4%)
    unnamed x4, waiting for transfers between devices  232 us
    reduce_scatter x1, waiting for transfers between devices, body(): lax.psum_scatter(jnp.dot(hidden, down_weight, preferred_element_type=jnp....  48.8 us
    all_gather x1, waiting for transfers between devices, body(): group_grad = lax.all_gather(out_grad, 'tensor', axis=0, tiled=True)  48.2 us
    unnamed x7, local copies, waits for them, and re-layouts  17 us
    dot_general x1, matrix products, body(): jnp.dot(hidden, down_weight, preferred_element_type=jnp.float32)  9.23 us
    dot_general x1, matrix products, body(): lax.dot_general(group_grad, down_weight, (((1,), (1,)), ((), ())), prefer...  9.07 us
    dot_general x1, matrix products, body(): lax.dot_general(group_grad, hidden, (((0,), (0,)), ((), ())), preferred_e...  8.87 us
  transfers between devices with their start and end apart: 3, of which 3 were waited for; matrix products, arithmetic and copies ran while one was open for 11% of the time, Pallas kernels for 0%

commit v1 on v0

v1 whole, which is shorter than its diff:
```python
import math

import jax
import jax.numpy as jnp
import numpy as np
from jax import lax
from jax.experimental import pallas as pl
from jax.experimental.pallas import tpu as pltpu
from jax.sharding import Mesh, PartitionSpec as P

BF = jnp.bfloat16
F32 = jnp.float32
AXES = ("z", "lo", "y", "hi", "core")
SIZES = dict(z=8, lo=2, y=4, hi=2, core=2)
D, HB, TOK, ROWS = 4608, 1152, 256, 16
COLS = 640
OUT_COLS = 288
WIDTHS = (256, 256, 256, 256, 128)
OFFSETS = tuple(sum(WIDTHS[:i]) for i in range(len(WIDTHS)))
Z_ORDER = (
    (0, 0), (1, 0), (0, 1), (1, 1), (0, 2), (1, 2), (2, 0), (0, 3), (1, 3),
    (3, 0), (2, 1), (4, 0), (3, 1), (2, 2), (4, 1), (3, 2), (2, 3), (4, 2), (3, 3), (4, 3),
)
WT = 512
COEFF = math.sqrt(2.0 / math.pi)


def gelu_and_slope(value):
    square = value * value
    tangent = jnp.tanh(COEFF * value * (1.0 + 0.044715 * square))
    gelu = 0.5 * value * (1.0 + tangent)
    slope = 0.5 * (1.0 + tangent) + 0.5 * value * (1.0 - tangent * tangent) * COEFF * (
        1.0 + 3.0 * 0.044715 * square
    )
    return gelu, slope


def z_plan():
    link, arrived, issue, done = 4.0, {}, {}, {}
    for chunk, hop in Z_ORDER:
        ready = 0.3 * chunk if hop == 0 else arrived[chunk, hop - 1]
        start = max(link, ready)
        link = start + 2.65 * WIDTHS[chunk] / 256 * (0.5 if hop == 3 else 1.0)
        arrived[chunk, hop] = link + 2.0
        issue[chunk, hop] = max(start - 3.0, ready)
        if hop == 3:
            done[chunk] = link + 2.0
    return issue, done


def kernel(
    gate, up, w, og, lout, ggrad, ugrad, dgrad,
    gv, uv, wv, hall, ogall, ogc, ogct, part, crecv, ysum, yhalf, yblk, hsend, hrecv, lov,
    gelu_s, us_s, ggv, guv, losend, lorecv, own, gdv, sems,
):
    idx = {a: lax.axis_index(a) for a in AXES}
    z, lo, y, hi, c = (idx[a] for a in AXES)
    count = [0]

    def sem():
        count[0] += 1
        return sems.at[count[0] - 1]

    def shifted(axis, delta):
        return lax.rem(idx[axis] + (delta % SIZES[axis]), SIZES[axis])

    def at(axis, delta):
        return {axis: shifted(axis, delta)}

    def local(src, dst):
        return pltpu.make_async_copy(src, dst, sem())

    sent = []

    def remote(src, dst, axis, delta):
        return pltpu.make_async_remote_copy(
            src_ref=src, dst_ref=dst, send_sem=sem(), recv_sem=sem(),
            device_id=at(axis, delta), device_id_type=pl.DeviceIdType.MESH,
        )

    def go(copy):
        copy.start()
        sent.append(copy)

    peers = [("z", d) for d in range(1, 8)] + [("lo", 1), ("y", 1), ("y", 3), ("hi", 1), ("core", 1)]
    barrier = pltpu.get_barrier_semaphore()
    for axis, delta in peers:
        pl.semaphore_signal(
            barrier, inc=1, device_id=at(axis, delta), device_id_type=pl.DeviceIdType.MESH
        )

    def chunk_cols(k):
        return pl.ds(OFFSETS[k], WIDTHS[k])

    loads = []
    for k in range(len(WIDTHS)):
        pair = (
            local(gate.at[:, chunk_cols(k)], gv.at[:, chunk_cols(k)]),
            local(up.at[:, chunk_cols(k)], uv.at[:, chunk_cols(k)]),
        )
        loads.append(pair)

    def window(zt):
        return pl.ds(pl.multiple_of(lax.div(zt * 9, 2) * 128, 128), COLS)

    load_og = local(og, ogall.at[y, hi, c])
    load_ogc = local(og.at[:, window(z)], ogc.at[y, hi, c, 0])
    load_w = [
        local(w.at[:, pl.ds(j * WT, WT)], wv.at[:, pl.ds(j * WT, WT)]) for j in range(D // WT)
    ]
    for pair in loads[:1]:
        pair[0].start()
        pair[1].start()
    load_og.start()
    load_ogc.start()
    for pair in loads[1:]:
        pair[0].start()
        pair[1].start()
    for copy in load_w:
        copy.start()

    def hidden(k):
        loads[k][0].wait()
        loads[k][1].wait()
        cols = chunk_cols(k)
        up_value = uv[:, cols].astype(F32)
        gelu, slope = gelu_and_slope(gv[:, cols].astype(F32))
        hall[pl.ds(0, TOK), cols] = (gelu * up_value).astype(BF)
        gelu_s[:, cols] = gelu
        us_s[:, cols] = up_value * slope

    steps = []

    def add(when, run):
        steps.append((when, len(steps), run))

    hidden(0)
    pl.semaphore_wait(barrier, len(peers))

    a2a = [
        remote(og.at[:, window(shifted("z", d))], ogc.at[y, hi, c, d], "z", d) for d in range(1, 8)
    ]

    class Gather:
        def __init__(self, buf):
            def move(yd, hd, axis, delta):
                ref = buf.at[shifted("y", yd), shifted("hi", hd), c]
                return remote(ref, ref, axis, delta)

            self.hi = move(0, 0, "hi", 1)
            self.right = [move(0, 0, "y", 1), move(0, 1, "y", 1), move(3, 0, "y", 1)]
            self.left = [move(0, 0, "y", 3), move(0, 1, "y", 3), move(1, 1, "y", 3)]
            self.core = {(yd, hd): move(yd, hd, "core", 1) for yd in range(4) for hd in range(2)}

        def schedule(self, t, first):
            def begin():
                first()
                go(self.right[0])
                go(self.left[0])
                go(self.hi)
                go(self.core[0, 0])

            def got_hi():
                self.hi.wait_recv()
                go(self.right[1])
                go(self.left[1])
                go(self.core[0, 1])

            def got_first():
                self.right[0].wait_recv()
                go(self.right[2])
                go(self.core[3, 0])
                self.left[0].wait_recv()
                go(self.core[1, 0])

            def got_second():
                self.left[1].wait_recv()
                go(self.left[2])
                go(self.core[1, 1])
                self.right[1].wait_recv()
                go(self.core[3, 1])

            def got_far():
                self.right[2].wait_recv()
                go(self.core[2, 0])
                self.left[2].wait_recv()
                go(self.core[2, 1])

            def finish():
                for copy in self.core.values():
                    copy.wait_recv()

            for when, run in zip(t, (begin, got_hi, got_first, got_second, got_far, finish)):
                add(when, run)

    rows = Gather(ogall)
    columns = Gather(ogc)

    def start_rows():
        load_og.wait()

    def start_columns():
        load_ogc.wait()
        for copy in a2a:
            copy.wait_recv()

    rows.schedule((0.01, 5.0, 5.5, 10.0, 15.0, 16.5), start_rows)
    columns.schedule((9.0, 14.0, 14.5, 19.0, 24.0, 25.5), start_columns)
    add(0.0, lambda: [go(copy) for copy in a2a])

    hops = {}
    for k in range(len(WIDTHS)):
        cols = chunk_cols(k)
        for hop in range(4):
            first, size = 256 * hop, 256
            if hop == 3:
                size = 128
            hops[k, hop, 0] = remote(
                hall.at[pl.ds(first, size), cols], hall.at[pl.ds(first + 256, size), cols], "z", 1
            )
            first = 0 if hop == 0 else 256 * (8 - hop)
            into = 256 * (7 - hop)
            if hop == 3:
                first, into = first + 128, into + 128
            hops[k, hop, 1] = remote(
                hall.at[pl.ds(first, size), cols], hall.at[pl.ds(into, size), cols], "z", 7
            )
    issue, done = z_plan()

    def z_step(k, hop):
        for way in range(2):
            if hop > 0:
                hops[k, hop - 1, way].wait_recv()
            go(hops[k, hop, way])

    for k, hop in Z_ORDER:
        add(issue[k, hop] + 0.02, lambda k=k, hop=hop: z_step(k, hop))
    for k in range(1, len(WIDTHS)):
        add(0.01 + 0.3 * (k - 1), lambda k=k: hidden(k))

    def forward(j):
        load_w[j].wait()
        cols = pl.ds(j * WT, WT)
        out = jnp.dot(hall[pl.ds(0, TOK), :], wv[:, cols], preferred_element_type=F32)
        part[:, :, :, :, cols] = out.astype(BF).reshape(4, 2, 2, ROWS, WT)

    for j in range(D // WT):
        add(1.8 + 0.5 * j, lambda j=j: forward(j))

    core_send = {}
    for yd in (2, 1, 3, 0):
        yy = shifted("y", yd)
        core_send[yd] = remote(part.at[yy, :, 1 - c], crecv.at[yy], "core", 1)
    y2 = shifted("y", 2)
    half_send = [
        remote(ysum.at[y2, 0], yhalf.at[0], "y", 1),
        remote(ysum.at[y2, 1], yhalf.at[1], "y", 3),
    ]
    blk_send = [
        remote(ysum.at[shifted("y", 1)], yblk.at[0], "y", 1),
        remote(ysum.at[shifted("y", 3)], yblk.at[1], "y", 3),
    ]
    hi_send = remote(hsend, hrecv, "hi", 1)
    store_lout = local(lov, lout)

    def scatter_core():
        for yd in (2, 1, 3, 0):
            go(core_send[yd])

    def scatter_far():
        core_send[2].wait_recv()
        ysum[y2] = (part[y2, :, c].astype(F32) + crecv[y2].astype(F32)).astype(BF)
        go(half_send[0])
        go(half_send[1])

    def scatter_near():
        for way in range(2):
            yd = 1 if way == 0 else 3
            yy = shifted("y", yd)
            core_send[yd].wait_recv()
            half_send[way].wait_recv()
            plain = 1 - way
            ysum[yy, plain] = (part[yy, plain, c].astype(F32) + crecv[yy, plain].astype(F32)).astype(BF)
            ysum[yy, way] = (
                part[yy, way, c].astype(F32) + crecv[yy, way].astype(F32) + yhalf[way].astype(F32)
            ).astype(BF)
            go(blk_send[way])

    def mine(hh):
        total = part[y, hh, c].astype(F32) + crecv[y, hh].astype(F32)
        return total + yblk[0, hh].astype(F32) + yblk[1, hh].astype(F32)

    def scatter_hi():
        core_send[0].wait_recv()
        blk_send[0].wait_recv()
        blk_send[1].wait_recv()
        hsend[...] = mine(1 - hi).astype(BF)
        go(hi_send)

    def scatter_end():
        hi_send.wait_recv()
        lov[...] = (mine(hi) + hrecv[...].astype(F32)).astype(BF)
        store_lout.start()

    add(7.5, scatter_core)
    add(10.5, scatter_far)
    add(15.5, scatter_near)
    add(24.0, scatter_hi)
    add(29.0, scatter_end)

    stores = []

    def backward(k):
        cols = chunk_cols(k)
        group = ogall[...].reshape(TOK, D)
        grad = lax.dot_general(
            group, wv[cols, :], (((1,), (1,)), ((), ())), preferred_element_type=F32
        )
        ggv[:, cols] = (grad * us_s[:, cols]).astype(BF)
        guv[:, cols] = (grad * gelu_s[:, cols]).astype(BF)
        for src, dst in ((ggv, ggrad), (guv, ugrad)):
            copy = local(src.at[:, cols], dst.at[:, cols])
            copy.start()
            stores.append(copy)

    for k in range(len(WIDTHS)):
        add(16.6 + 0.8 * k, lambda k=k: backward(k))

    def transpose(s):
        block = ogc[:, :, :, s].reshape(TOK, COLS)
        ogct[:, pl.ds(TOK * s, TOK)] = block.T

    for s in range(8):
        add(25.6 + 0.2 * s, lambda s=s: transpose(s))

    first_row = pl.multiple_of(64 * lax.rem(z, 2), 64)
    lo_send = [
        remote(losend.at[:, chunk_cols(k)], lorecv.at[:, chunk_cols(k)], "lo", 1)
        for k in range(len(WIDTHS))
    ]

    def weight_grad(k):
        cols = chunk_cols(k)
        for way in range(2):
            hops[k, 3, way].wait_recv()
        total = jnp.dot(
            ogct[pl.ds(first_row, 2 * OUT_COLS), :], hall[:, cols], preferred_element_type=F32
        )
        low, high = total[:OUT_COLS], total[OUT_COLS:]
        losend[:, cols] = jnp.where(lo == 0, high, low).astype(BF)
        go(lo_send[k])
        own[:, cols] = jnp.where(lo == 0, low, high)

    def weight_end(k):
        cols = chunk_cols(k)
        lo_send[k].wait_recv()
        total = own[:, cols] + lorecv[:, cols].astype(F32)
        total = jnp.concatenate([total, jnp.zeros((96, WIDTHS[k]), F32)], axis=0)
        gdv[cols, :] = total.T[:, :OUT_COLS].astype(BF)
        copy = local(gdv.at[cols], dgrad.at[cols])
        copy.start()
        stores.append(copy)

    free = 27.3
    for k in range(len(WIDTHS)):
        free = max(free, done[k]) + 0.05
        add(free, lambda k=k: weight_grad(k))
        free += 0.4
    prev = 0.0
    for k in range(len(WIDTHS)):
        prev = max(prev, max(27.3, done[k])) + 5.5 * WIDTHS[k] / 256
        add(prev, lambda k=k: weight_end(k))

    for _, _, run in sorted(steps, key=lambda item: item[:2]):
        run()
    for copy in sent:
        copy.wait_send()
    store_lout.wait()
    for copy in stores:
        copy.wait()


def body(gate, up, w, og):
    any_spec = pl.BlockSpec(memory_space=pl.ANY)
    shapes = (
        jax.ShapeDtypeStruct((ROWS, D), BF),
        jax.ShapeDtypeStruct((TOK, HB), BF),
        jax.ShapeDtypeStruct((TOK, HB), BF),
        jax.ShapeDtypeStruct((HB, OUT_COLS), BF),
    )
    v = pltpu.VMEM
    scratch = [
        v((TOK, HB), BF), v((TOK, HB), BF), v((HB, D), BF),
        v((8 * TOK, HB), BF), v((4, 2, 2, ROWS, D), BF), v((4, 2, 2, 8, ROWS, COLS), BF),
        v((COLS, 8 * TOK), BF),
        v((4, 2, 2, ROWS, D), BF), v((4, 2, ROWS, D), BF), v((4, 2, ROWS, D), BF),
        v((2, ROWS, D), BF), v((2, 2, ROWS, D), BF), v((ROWS, D), BF), v((ROWS, D), BF), v((ROWS, D), BF),
        v((TOK, HB), F32), v((TOK, HB), F32), v((TOK, HB), BF), v((TOK, HB), BF),
        v((OUT_COLS, HB), BF), v((OUT_COLS, HB), BF), v((OUT_COLS, HB), F32), v((HB, OUT_COLS), BF),
        pltpu.SemaphoreType.DMA((256,)),
    ]
    return pl.pallas_call(
        kernel,
        out_shape=shapes,
        in_specs=[any_spec] * 4,
        out_specs=(any_spec,) * 4,
        scratch_shapes=scratch,
        compiler_params=pltpu.CompilerParams(
            collective_id=0, has_side_effects=True, vmem_limit_bytes=60 * 2**20
        ),
        cost_estimate=pl.CostEstimate(
            flops=6 * TOK * HB * D, bytes_accessed=14_000_000, transcendentals=TOK * HB
        ),
        name="geglu_down",
    )(gate, up, w, og)


def solution(mesh):
    fine = Mesh(mesh.devices.reshape(tuple(SIZES[a] for a in AXES)), AXES)
    dp, tensor = ("z", "lo"), ("y", "hi", "core")
    return jax.shard_map(
        body,
        mesh=fine,
        in_specs=(P(dp, tensor), P(dp, tensor), P(tensor, None), P(dp + tensor, None)),
        out_specs=(P(dp + tensor, None), P(dp, tensor), P(dp, tensor), P(tensor, dp)),
        check_vma=False,
    )
```

time: 389 us -> 83.3 us (0.21)
  waiting for transfers between devices: 329 us -> 0 us
  Pallas kernels: 0 us -> 74.4 us
  matrix products: 27.2 us -> 0 us
  between operations: 13.7 us -> 0.64 us
  local copies, waits for them, and re-layouts: 17 us -> 7.71 us
    unnamed x4 -> x0, waiting for transfers between devices: 232 us -> none
    pallas_call x0 -> x1, Pallas kernels: none -> 74.4 us  [body(): pl.pallas_call(kernel, out_shape=shapes, in_specs=[any_spec] * 4, out_spe...]
    reduce_scatter x1 -> x0, waiting for transfers between devices: 48.8 us -> none  [body(): lax.psum_scatter(jnp.dot(hidden, down_weight, preferred_element_type=jnp....]
    all_gather x1 -> x0, waiting for transfers between devices: 48.2 us -> none  [body(): group_grad = lax.all_gather(out_grad, 'tensor', axis=0, tiled=True)]
    dot_general x3 -> x0, matrix products: 27.2 us -> none  [the longest x1 9.23 us: body(): jnp.dot(hidden, down_weight, preferred_element_type=jnp.float32)]
    unnamed x7 -> x3, local copies, waits for them, and re-layouts: 17 us -> 5.42 us
  transfers between devices with their start and end apart: 3 -> 0, of which waited for: 3 -> 0; matrix products, arithmetic and copies ran while one was open for 11% -> 0% of each run, Pallas kernels for 0% -> 0%
where the time goes in v1:
time: 83.3 us; the launch traced here: 82.8 us
  Pallas kernels  74.4 us (89%)
  local copies, waits for them, and re-layouts  7.71 us (9%)
    pallas_call x1, Pallas kernels, body(): pl.pallas_call(kernel, out_shape=shapes, in_specs=[any_spec] * 4, out_spe...  74.4 us
    unnamed x3, local copies, waits for them, and re-layouts  5.42 us
    pallas_call x1, local copies, waits for them, and re-layouts, body(): pl.pallas_call(kernel, out_shape=shapes, in_specs=[any_spec] * 4, out_spe...  2.29 us

profile of v1, /device:TPU:16, one launch (start us, length us, event | category | flops | bytes accessed | tf_op | source)
XLA Modules:
  0.0 82.8 jit_solution(1438002871703135069)
XLA Ops:
  0.6 74.4 %geglu_down.1 = (bf16[16,4608]{1,0:T(8,128)(2,1)}, bf16[256,1152]{1,0:T(8,128)(2,1)}, bf16[256,1152]{1,0:T(8,128)(2,1)}, bf16[1152,288]{1,0:T(8,128)(2,1)}) custom-call(bf16[256,1152]{1,0:T(8,128)(2,1)} %gate.1, bf16[256,1152]{1,0:T(8,128)(2,1)} %up.1, bf16[1152,4608]{1,0:T(8,128)(2,1)} %w.1, bf16[16,4608]{1,0:T(8,128)(2,1)} %og.1), custom_call_target="tpu_custom_call" | custom-call | flops 8153726976 | bytes 14000000 | tf_op jit(solution)/shard_map/geglu_down/pallas_call | solution.py:402
  75.0 2.3 %copy.8 = bf16[1152,288]{0,1:T(8,128)(2,1)} copy(bf16[1152,288]{1,0:T(8,128)(2,1)} %get-tuple-element.7) | data formatting | bytes 1327104 | tf_op jit(solution)/shard_map/geglu_down/pallas_call | solution.py:402
  77.3 1.6 %copy.12 = bf16[16,4608]{1,0:T(8,128)(2,1)} copy(bf16[16,4608]{1,0:T(8,128)(2,1)} %get-tuple-element.12) | data formatting | bytes 294912
  78.9 1.9 %copy.13 = bf16[256,1152]{1,0:T(8,128)(2,1)} copy(bf16[256,1152]{1,0:T(8,128)(2,1)} %get-tuple-element.13) | data formatting | bytes 1179648
  80.8 1.9 %copy.14 = bf16[256,1152]{1,0:T(8,128)(2,1)} copy(bf16[256,1152]{1,0:T(8,128)(2,1)} %get-tuple-element.14) | data formatting | bytes 1179648

commit v2 on v1

v2 whole, which is shorter than its diff:
```python
import math

import jax
import jax.numpy as jnp
from jax import lax
from jax.experimental import pallas as pl
from jax.experimental.pallas import tpu as pltpu
from jax.sharding import Mesh, PartitionSpec as P

BF = jnp.bfloat16
F32 = jnp.float32
AXES = ("z", "lo", "y", "hi", "core")
SIZES = dict(z=8, lo=2, y=4, hi=2, core=2)
D, HB, TOK, ROWS = 4608, 1152, 256, 16
COLS = 640
OUT_COLS = 288
WIDTHS = (384, 384, 128, 128, 128)
OFFSETS = tuple(sum(WIDTHS[:i]) for i in range(len(WIDTHS)))
Z_ORDER = (
    (0, 0), (1, 0), (0, 1), (1, 1), (0, 2), (1, 2), (0, 3), (2, 0), (1, 3), (3, 0),
    (2, 1), (4, 0), (3, 1), (2, 2), (4, 1), (3, 2), (2, 3), (4, 2), (3, 3), (4, 3),
)
WT = 512
COEFF = math.sqrt(2.0 / math.pi)


def gelu_and_slope(value):
    square = value * value
    tangent = jnp.tanh(COEFF * value * (1.0 + 0.044715 * square))
    gelu = 0.5 * value * (1.0 + tangent)
    slope = 0.5 * (1.0 + tangent) + 0.5 * value * (1.0 - tangent * tangent) * COEFF * (
        1.0 + 3.0 * 0.044715 * square
    )
    return gelu, slope


LANES = dict(z=(20.2, 2.0), y=(20.2, 2.6), x=(20.2, 2.6), core=(4.0, 2.0))


class Move:
    def __init__(self, copy, lane, src, hops=1):
        self.dma, self.lane, self.landed = copy, lane, None
        rate, self.lag = LANES[lane.rstrip("+-")]
        self.busy = rate * math.prod(src.shape) * 2e-6 * hops
        self.lag += 0.6 * (hops - 1)


class Steps:
    def __init__(self):
        self.items = {}

    def add(self, key, rank, act=None, waits=(), starts=(), after=(), cost=0.0):
        self.items[key] = (rank, act, tuple(waits), tuple(starts), tuple(after), cost)

    def order(self):
        now, idle, left, done, out = 0.0, {}, dict(self.items), set(), []
        while left:
            best = None
            for key, (rank, _, waits, _, after, _) in left.items():
                if any(k not in done for k in after) or any(m.landed is None for m in waits):
                    continue
                ready = max([now] + [m.landed for m in waits])
                choice = (ready, rank, key)
                if best is None or choice[:2] < best[:2]:
                    best = choice
            ready, _, key = best
            _, _, _, starts, _, cost = left.pop(key)
            now = ready + cost
            for move in starts:
                now += 0.05
                begin = max(now, idle.get(move.lane, 0.0))
                idle[move.lane] = begin + move.busy
                move.landed = idle[move.lane] + move.lag
            done.add(key)
            out.append((ready, now, key))
        return out

    def emit(self):
        sent = []
        for _, _, key in self.order():
            _, act, waits, starts, _, _ = self.items[key]
            for move in waits:
                move.dma.wait_recv()
            if act is not None:
                act()
            for move in starts:
                move.dma.start()
                sent.append(move)
        for move in sent:
            move.dma.wait_send()


def kernel(
    gate, up, w, og, lout, ggrad, ugrad, dgrad,
    gv, uv, wv, hall, ogall, ogc, ogct, part, crecv, ysum, yhalf, yblk, hsend, hrecv, lov,
    gelu_s, us_s, ggv, guv, acc, losend, lorecv, own, gdv, sems,
):
    idx = {a: lax.axis_index(a) for a in AXES}
    z, lo, y, hi, c = (idx[a] for a in AXES)
    count = [0]

    def sem():
        count[0] += 1
        return sems.at[count[0] - 1]

    def shifted(axis, delta):
        return lax.rem(idx[axis] + (delta % SIZES[axis]), SIZES[axis])

    def at(axis, delta):
        return {axis: shifted(axis, delta)}

    def local(src, dst):
        return pltpu.make_async_copy(src, dst, sem())

    def remote(src, dst, axis, delta):
        copy = pltpu.make_async_remote_copy(
            src_ref=src, dst_ref=dst, send_sem=sem(), recv_sem=sem(),
            device_id=at(axis, delta), device_id_type=pl.DeviceIdType.MESH,
        )
        lane, hops = axis, 1
        if axis in ("hi", "lo"):
            lane = "x"
        elif axis in ("z", "y"):
            hops = min(delta, SIZES[axis] - delta)
            lane = axis + ("+" if delta == hops else "-")
        return Move(copy, lane, src, hops)

    peers = [("z", d) for d in range(1, 8)] + [("lo", 1), ("y", 1), ("y", 3), ("hi", 1), ("core", 1)]
    barrier = pltpu.get_barrier_semaphore()
    for axis, delta in peers:
        pl.semaphore_signal(
            barrier, inc=1, device_id=at(axis, delta), device_id_type=pl.DeviceIdType.MESH
        )

    def chunk_cols(k):
        return pl.ds(OFFSETS[k], WIDTHS[k])

    loads = []
    for k in range(len(WIDTHS)):
        pair = (
            local(gate.at[:, chunk_cols(k)], gv.at[:, chunk_cols(k)]),
            local(up.at[:, chunk_cols(k)], uv.at[:, chunk_cols(k)]),
        )
        loads.append(pair)

    def window(zt):
        return pl.ds(pl.multiple_of(lax.div(zt * 9, 2) * 128, 128), COLS)

    load_og = local(og, ogall.at[y, hi, c])
    load_ogc = local(og.at[:, window(z)], ogc.at[y, hi, c, 0])
    load_w = [
        local(w.at[:, pl.ds(j * WT, WT)], wv.at[:, pl.ds(j * WT, WT)]) for j in range(D // WT)
    ]
    for pair in loads[:1]:
        pair[0].start()
        pair[1].start()
    load_og.start()
    load_ogc.start()
    for pair in loads[1:]:
        pair[0].start()
        pair[1].start()
    for copy in load_w:
        copy.start()

    def hidden(k):
        loads[k][0].wait()
        loads[k][1].wait()
        cols = chunk_cols(k)
        up_value = uv[:, cols].astype(F32)
        gelu, slope = gelu_and_slope(gv[:, cols].astype(F32))
        hall[pl.ds(0, TOK), cols] = (gelu * up_value).astype(BF)
        gelu_s[:, cols] = gelu
        us_s[:, cols] = up_value * slope

    steps = Steps()
    add = steps.add
    chunks = range(len(WIDTHS))
    hidden(0)
    hidden(1)
    pl.semaphore_wait(barrier, len(peers))

    a2a = [
        remote(og.at[:, window(shifted("z", d))], ogc.at[y, hi, c, d], "z", d) for d in range(1, 8)
    ]
    add("columns out", 0, starts=a2a)

    def gather(name, buf, rank, act, waits, after, later):
        def move(yd, hd, axis, delta):
            ref = buf.at[shifted("y", yd), shifted("hi", hd), c]
            return remote(ref, ref, axis, delta)

        across = move(0, 0, "hi", 1)
        right = [move(0, 0, "y", 1), move(0, 1, "y", 1), move(3, 0, "y", 1)]
        left = [move(0, 0, "y", 3), move(0, 1, "y", 3), move(1, 1, "y", 3)]
        core = {(yd, hd): move(yd, hd, "core", 1) for yd in range(4) for hd in range(2)}

        def part(i, wait, *starts):
            add((name, i), rank, waits=(wait,), starts=starts, after=later.get(i, ()))

        add((name, 0), rank, act, waits, (right[0], left[0], across, core[0, 0]), after)
        part(1, across, right[1], left[1], core[0, 1])
        part(2, right[0], right[2], core[3, 0])
        part(3, left[0], core[1, 0])
        part(4, left[1], left[2], core[1, 1])
        part(5, right[1], core[3, 1])
        part(6, right[2], core[2, 0])
        part(7, left[2], core[2, 1])
        add((name, 8), rank, waits=core.values(), after=[(name, i) for i in range(8)])

    first_columns = {i: [("columns", 2), ("columns", 4)] for i in (2, 4)}
    gather("rows", ogall, 3, load_og.wait, (), ("columns out",), first_columns)
    gather("columns", ogc, 2, load_ogc.wait, a2a, (), {})

    hops = {}
    for k in chunks:
        cols = chunk_cols(k)
        for hop in range(4):
            first, size = 256 * hop, 256
            if hop == 3:
                size = 128
            hops[k, hop, 0] = remote(
                hall.at[pl.ds(first, size), cols], hall.at[pl.ds(first + 256, size), cols], "z", 1
            )
            first = 0 if hop == 0 else 256 * (8 - hop)
            into = 256 * (7 - hop)
            if hop == 3:
                first, into = first + 128, into + 128
            hops[k, hop, 1] = remote(
                hall.at[pl.ds(first, size), cols], hall.at[pl.ds(into, size), cols], "z", 7
            )
    for i, (k, hop) in enumerate(Z_ORDER):
        for way in range(2):
            after = [("z", *Z_ORDER[i - 1], way)] if i else ["columns out"]
            if hop == 0 and k > 1:
                after.append(("hidden", k))
            waits = (hops[k, hop - 1, way],) if hop else ()
            add(("z", k, hop, way), 1, waits=waits, starts=(hops[k, hop, way],), after=after)
    for k in chunks[2:]:
        add(("hidden", k), 4, lambda k=k: hidden(k), after=[("rows", 0)], cost=0.9 * WIDTHS[k] / 256)

    def forward(j):
        load_w[j].wait()
        cols = pl.ds(j * WT, WT)
        out = jnp.dot(hall[pl.ds(0, TOK), :], wv[:, cols], preferred_element_type=F32)
        part[:, :, :, :, cols] = out.astype(BF).reshape(4, 2, 2, ROWS, WT)

    tiles = range(D // WT)
    for j in tiles:
        add(("forward", j), 5, lambda j=j: forward(j), after=[("hidden", k) for k in chunks[2:]], cost=0.6)

    core_send = {}
    for yd in (2, 1, 3, 0):
        yy = shifted("y", yd)
        core_send[yd] = remote(part.at[yy, :, 1 - c], crecv.at[yy], "core", 1)
    y2 = shifted("y", 2)
    half_send = [
        remote(ysum.at[y2, 0], yhalf.at[0], "y", 1),
        remote(ysum.at[y2, 1], yhalf.at[1], "y", 3),
    ]
    blk_send = [
        remote(ysum.at[shifted("y", 1)], yblk.at[0], "y", 1),
        remote(ysum.at[shifted("y", 3)], yblk.at[1], "y", 3),
    ]
    hi_send = remote(hsend, hrecv, "hi", 1)
    store_lout = local(lov, lout)

    def scatter_far():
        ysum[y2] = (part[y2, :, c].astype(F32) + crecv[y2].astype(F32)).astype(BF)

    def scatter_near(way):
        yy = shifted("y", 1 if way == 0 else 3)
        plain = 1 - way
        ysum[yy, plain] = (part[yy, plain, c].astype(F32) + crecv[yy, plain].astype(F32)).astype(BF)
        ysum[yy, way] = (
            part[yy, way, c].astype(F32) + crecv[yy, way].astype(F32) + yhalf[way].astype(F32)
        ).astype(BF)

    def mine(hh):
        total = part[y, hh, c].astype(F32) + crecv[y, hh].astype(F32)
        return total + yblk[0, hh].astype(F32) + yblk[1, hh].astype(F32)

    def scatter_hi():
        hsend[...] = mine(1 - hi).astype(BF)

    def scatter_end():
        lov[...] = (mine(hi) + hrecv[...].astype(F32)).astype(BF)
        store_lout.start()

    add("scatter core", 3, starts=core_send.values(), after=[("forward", j) for j in tiles])
    add("scatter far", 3, scatter_far, (core_send[2],), half_send, cost=0.3)
    for way in range(2):
        waits = (core_send[1 + 2 * way], half_send[way])
        add(("near", way), 3, lambda way=way: scatter_near(way), waits, (blk_send[way],), [("rows", 2), ("rows", 4)], cost=0.3)
    add("scatter hi", 3, scatter_hi, (core_send[0], *blk_send), (hi_send,), cost=0.2)
    add("scatter end", 3, scatter_end, (hi_send,), cost=0.2)

    stores = []

    def backward(k):
        cols = chunk_cols(k)
        group = ogall[...].reshape(TOK, D)
        grad = lax.dot_general(
            group, wv[cols, :], (((1,), (1,)), ((), ())), preferred_element_type=F32
        )
        ggv[:, cols] = (grad * us_s[:, cols]).astype(BF)
        guv[:, cols] = (grad * gelu_s[:, cols]).astype(BF)
        for src, dst in ((ggv, ggrad), (guv, ugrad)):
            copy = local(src.at[:, cols], dst.at[:, cols])
            copy.start()
            stores.append(copy)

    for k in chunks:
        add(("backward", k), 6, lambda k=k: backward(k), after=[("rows", 8)], cost=1.1 * WIDTHS[k] / 256)

    def transpose(s):
        block = ogc[:, :, :, s].reshape(TOK, COLS)
        ogct[:, pl.ds(TOK * s, TOK)] = block.T

    for s in range(8):
        add(("transpose", s), 2, lambda s=s: transpose(s), after=[("columns", 8)], cost=0.25)

    first_row = pl.multiple_of(64 * lax.rem(z, 2), 64)
    window_rows = pl.ds(first_row, 2 * OUT_COLS)
    lo_send = [
        remote(losend.at[:, chunk_cols(k)], lorecv.at[:, chunk_cols(k)], "lo", 1) for k in chunks
    ]

    def product(k, first, size):
        return jnp.dot(
            ogct[window_rows, pl.ds(first, size)], hall[pl.ds(first, size), chunk_cols(k)],
            preferred_element_type=F32,
        )

    def weight_most(k):
        acc[:, chunk_cols(k)] = product(k, 0, 1024) + product(k, 1280, 768)

    def weight_last(k):
        cols = chunk_cols(k)
        total = acc[:, cols] + product(k, 1024, 256)
        low, high = total[:OUT_COLS], total[OUT_COLS:]
        losend[:, cols] = jnp.where(lo == 0, high, low).astype(BF)
        own[:, cols] = jnp.where(lo == 0, low, high)

    def weight_end(k):
        cols = chunk_cols(k)
        gdv[:, cols] = (own[:, cols] + lorecv[:, cols].astype(F32)).astype(BF)
        copy = local(gdv.at[:, cols], dgrad.at[:, cols])
        copy.start()
        stores.append(copy)

    transposed = [("transpose", s) for s in range(8)]
    for k in chunks:
        after = transposed + [("z", k, 3, 0), ("z", k, 3, 1)]
        size = (WIDTHS[k] + 255) // 256
        add(("most", k), 2, lambda k=k: weight_most(k), after=after, cost=0.75 * size)
        add(
            ("last", k), 1, lambda k=k: weight_last(k), (hops[k, 3, 0], hops[k, 3, 1]),
            (lo_send[k],), [("most", k)], 0.3 * size,
        )
        add(("end", k), 3, lambda k=k: weight_end(k), (lo_send[k],), cost=0.2 * size)

    steps.emit()
    store_lout.wait()
    for copy in stores:
        copy.wait()


def body(gate, up, w, og):
    any_spec = pl.BlockSpec(memory_space=pl.ANY)
    shapes = (
        jax.ShapeDtypeStruct((ROWS, D), BF),
        jax.ShapeDtypeStruct((TOK, HB), BF),
        jax.ShapeDtypeStruct((TOK, HB), BF),
        jax.ShapeDtypeStruct((OUT_COLS, HB), BF),
    )
    v = pltpu.VMEM
    scratch = [
        v((TOK, HB), BF), v((TOK, HB), BF), v((HB, D), BF),
        v((8 * TOK, HB), BF), v((4, 2, 2, ROWS, D), BF), v((4, 2, 2, 8, ROWS, COLS), BF),
        v((COLS, 8 * TOK), BF),
        v((4, 2, 2, ROWS, D), BF), v((4, 2, ROWS, D), BF), v((4, 2, ROWS, D), BF),
        v((2, ROWS, D), BF), v((2, 2, ROWS, D), BF), v((ROWS, D), BF), v((ROWS, D), BF), v((ROWS, D), BF),
        v((TOK, HB), F32), v((TOK, HB), F32), v((TOK, HB), BF), v((TOK, HB), BF),
        v((2 * OUT_COLS, HB), F32),
        v((OUT_COLS, HB), BF), v((OUT_COLS, HB), BF), v((OUT_COLS, HB), F32), v((OUT_COLS, HB), BF),
        pltpu.SemaphoreType.DMA((256,)),
    ]
    results = pl.pallas_call(
        kernel,
        out_shape=shapes,
        in_specs=[any_spec] * 4,
        out_specs=(any_spec,) * 4,
        scratch_shapes=scratch,
        compiler_params=pltpu.CompilerParams(
            collective_id=0, has_side_effects=True, vmem_limit_bytes=60 * 2**20
        ),
        cost_estimate=pl.CostEstimate(
            flops=6 * TOK * HB * D, bytes_accessed=14_000_000, transcendentals=TOK * HB
        ),
        name="geglu_down",
    )(gate, up, w, og)
    layer_out, grad_gate, grad_up, grad_down = finish(results)
    return layer_out, grad_gate, grad_up, grad_down.T


def finish_kernel(*refs):
    n = len(refs) // 3
    sources, targets, held = refs[:n], refs[n : 2 * n], refs[2 * n : 3 * n]
    sems = refs[3 * n]
    moves = []
    for source, target, mid in zip(sources, targets, held):
        rows = source.shape[0]
        pieces = 1 if rows < 128 else 4 if rows % 64 == 0 else 3
        for piece in range(pieces):
            part = pl.ds(piece * (rows // pieces), rows // pieces)
            k = len(moves)
            moves.append(
                (
                    pltpu.make_async_copy(source.at[part], mid.at[part], sems.at[0, k]),
                    pltpu.make_async_copy(mid.at[part], target.at[part], sems.at[1, k]),
                )
            )
    for first, _ in moves:
        first.start()
    for first, second in moves:
        first.wait()
        second.start()
    for _, second in moves:
        second.wait()


def finish(results):
    any_spec = pl.BlockSpec(memory_space=pl.ANY)
    n = len(results)
    return pl.pallas_call(
        finish_kernel,
        out_shape=tuple(jax.ShapeDtypeStruct(r.shape, r.dtype) for r in results),
        in_specs=[any_spec] * n,
        out_specs=(any_spec,) * n,
        scratch_shapes=[pltpu.VMEM(r.shape, r.dtype) for r in results]
        + [pltpu.SemaphoreType.DMA((2, 4 * n))],
        compiler_params=pltpu.CompilerParams(vmem_limit_bytes=60 * 2**20),
        name="finish",
    )(*results)


def solution(mesh):
    fine = Mesh(mesh.devices.reshape(tuple(SIZES[a] for a in AXES)), AXES)
    dp, tensor = ("z", "lo"), ("y", "hi", "core")
    return jax.shard_map(
        body,
        mesh=fine,
        in_specs=(P(dp, tensor), P(dp, tensor), P(tensor, None), P(dp + tensor, None)),
        out_specs=(P(dp + tensor, None), P(dp, tensor), P(dp, tensor), P(tensor, dp)),
        check_vma=False,
    )
```

time: 83.3 us -> 72.9 us (0.88)
  local copies, waits for them, and re-layouts: 7.71 us -> 0 us
  Pallas kernels: 74.4 us -> 72.1 us
    unnamed x3 -> x0, local copies, waits for them, and re-layouts: 5.42 us -> none
    pallas_call x1, Pallas kernels: 74.4 us -> 69.6 us  [body(): pl.pallas_call(kernel, out_shape=shapes, in_specs=[any_spec] * 4, out_spe...]
    pallas_call x0 -> x1, Pallas kernels: none -> 2.57 us  [finish(): pl.pallas_call(finish_kernel, out_shape=tuple((jax.ShapeDtypeStruct(r.sha...]
    pallas_call x1 -> x0, local copies, waits for them, and re-layouts: 2.29 us -> none  [body(): pl.pallas_call(kernel, out_shape=shapes, in_specs=[any_spec] * 4, out_spe...]
where the time goes in v2:
time: 72.9 us; the launch traced here: 72.8 us
  Pallas kernels  72.1 us (99%)
    pallas_call x1, Pallas kernels, body(): pl.pallas_call(kernel, out_shape=shapes, in_specs=[any_spec] * 4, out_spe...  69.6 us
    pallas_call x1, Pallas kernels, finish(): pl.pallas_call(finish_kernel, out_shape=tuple((jax.ShapeDtypeStruct(r.sha...  2.57 us

profile of v2, /device:TPU:16, one launch (start us, length us, event | category | flops | bytes accessed | tf_op | source)
XLA Modules:
  0.0 72.8 jit_solution(6947306212628507388)
XLA Ops:
  0.6 69.6 %geglu_down.1 = (bf16[16,4608]{1,0:T(8,128)(2,1)}, bf16[256,1152]{1,0:T(8,128)(2,1)}, bf16[256,1152]{1,0:T(8,128)(2,1)}, bf16[288,1152]{1,0:T(8,128)(2,1)}) custom-call(bf16[256,1152]{1,0:T(8,128)(2,1)} %gate.1, bf16[256,1152]{1,0:T(8,128)(2,1)} %up.1, bf16[1152,4608]{1,0:T(8,128)(2,1)} %w.1, bf16[16,4608]{1,0:T(8,128)(2,1)} %og.1), custom_call_target="tpu_custom_call" | custom-call | flops 8153726976 | bytes 14000000 | tf_op jit(solution)/shard_map/geglu_down/pallas_call | solution.py:388
  70.2 2.6 %finish.1 = (bf16[16,4608]{1,0:T(8,128)(2,1)}, bf16[256,1152]{1,0:T(8,128)(2,1)}, bf16[256,1152]{1,0:T(8,128)(2,1)}, bf16[288,1152]{1,0:T(8,128)(2,1)}) custom-call(bf16[16,4608]{1,0:T(8,128)(2,1)} %get-tuple-element.12.refs_0_, bf16[256,1152]{1,0:T(8,128)(2,1)} %get-tuple-element.13.refs_1_, bf16[256,1152]{1,0:T(8,128)(2,1)} %get-tuple-element.14.refs_2_, ...), custom_call_target="tpu_custom_call" | custom-call | tf_op jit(solution)/shard_map/finish/pallas_call | solution.py:435

commit v3 on v2

--- a/solution.py
+++ b/solution.py
@@ -14,12 +14,9 @@
 D, HB, TOK, ROWS = 4608, 1152, 256, 16
 COLS = 640
 OUT_COLS = 288
-WIDTHS = (384, 384, 128, 128, 128)
+WIDTHS = (256, 256, 256, 128, 128, 128)
 OFFSETS = tuple(sum(WIDTHS[:i]) for i in range(len(WIDTHS)))
-Z_ORDER = (
-    (0, 0), (1, 0), (0, 1), (1, 1), (0, 2), (1, 2), (0, 3), (2, 0), (1, 3), (3, 0),
-    (2, 1), (4, 0), (3, 1), (2, 2), (4, 1), (3, 2), (2, 3), (4, 2), (3, 3), (4, 3),
-)
+Z_ORDER = ((3, 0), (2, 0), (1, 0), (0, 0), (2, 1), (0, 1), (1, 1), (5, 0), (4, 0), (2, 2), (5, 1), (4, 1), (2, 3), (0, 2), (1, 2), (0, 3), (4, 2), (3, 1), (1, 3), (5, 2), (4, 3), (3, 2), (5, 3), (3, 3))
 WT = 512
 COEFF = math.sqrt(2.0 / math.pi)
 
@@ -175,8 +172,6 @@
     steps = Steps()
     add = steps.add
     chunks = range(len(WIDTHS))
-    hidden(0)
-    hidden(1)
     pl.semaphore_wait(barrier, len(peers))
 
     a2a = [
@@ -231,12 +226,15 @@
     for i, (k, hop) in enumerate(Z_ORDER):
         for way in range(2):
             after = [("z", *Z_ORDER[i - 1], way)] if i else ["columns out"]
-            if hop == 0 and k > 1:
+            if hop == 0:
                 after.append(("hidden", k))
             waits = (hops[k, hop - 1, way],) if hop else ()
             add(("z", k, hop, way), 1, waits=waits, starts=(hops[k, hop, way],), after=after)
-    for k in chunks[2:]:
-        add(("hidden", k), 4, lambda k=k: hidden(k), after=[("rows", 0)], cost=0.9 * WIDTHS[k] / 256)
+    for k in chunks:
+        add(
+            ("hidden", k), 0 if k < 2 else 4, lambda k=k: hidden(k), cost=0.9 * WIDTHS[k] / 256,
+            after=[("hidden", k - 1) if k else "columns out"],
+        )
 
     def forward(j):
         load_w[j].wait()
@@ -246,7 +244,7 @@
 
     tiles = range(D // WT)
     for j in tiles:
-        add(("forward", j), 5, lambda j=j: forward(j), after=[("hidden", k) for k in chunks[2:]], cost=0.6)
+        add(("forward", j), 5, lambda j=j: forward(j), after=[("hidden", k) for k in chunks], cost=0.6)
 
     core_send = {}
     for yd in (2, 1, 3, 0):

time: 72.9 us -> 70.7 us (0.970)
  Pallas kernels: 72.1 us -> 69.8 us
    pallas_call x1, Pallas kernels: 69.6 us -> 67.3 us  [body(): pl.pallas_call(kernel, out_shape=shapes, in_specs=[any_spec] * 4, out_spe...]
where the time goes in v3:
time: 70.7 us; the launch traced here: 70.5 us
  Pallas kernels  69.8 us (99%)
    pallas_call x1, Pallas kernels, body(): pl.pallas_call(kernel, out_shape=shapes, in_specs=[any_spec] * 4, out_spe...  67.3 us
    pallas_call x1, Pallas kernels, finish(): pl.pallas_call(finish_kernel, out_shape=tuple((jax.ShapeDtypeStruct(r.sha...  2.57 us

profile of v3, /device:TPU:16, one launch (start us, length us, event | category | flops | bytes accessed | tf_op | source)
XLA Modules:
  0.0 70.5 jit_solution(18394838019413248980)
XLA Ops:
  0.6 67.3 %geglu_down.1 = (bf16[16,4608]{1,0:T(8,128)(2,1)}, bf16[256,1152]{1,0:T(8,128)(2,1)}, bf16[256,1152]{1,0:T(8,128)(2,1)}, bf16[288,1152]{1,0:T(8,128)(2,1)}) custom-call(bf16[256,1152]{1,0:T(8,128)(2,1)} %gate.1, bf16[256,1152]{1,0:T(8,128)(2,1)} %up.1, bf16[1152,4608]{1,0:T(8,128)(2,1)} %w.1, bf16[16,4608]{1,0:T(8,128)(2,1)} %og.1), custom_call_target="tpu_custom_call" | custom-call | flops 8153726976 | bytes 14000000 | tf_op jit(solution)/shard_map/geglu_down/pallas_call | solution.py:386
  67.9 2.6 %finish.1 = (bf16[16,4608]{1,0:T(8,128)(2,1)}, bf16[256,1152]{1,0:T(8,128)(2,1)}, bf16[256,1152]{1,0:T(8,128)(2,1)}, bf16[288,1152]{1,0:T(8,128)(2,1)}) custom-call(bf16[16,4608]{1,0:T(8,128)(2,1)} %get-tuple-element.12.refs_0_, bf16[256,1152]{1,0:T(8,128)(2,1)} %get-tuple-element.13.refs_1_, bf16[256,1152]{1,0:T(8,128)(2,1)} %get-tuple-element.14.refs_2_, ...), custom_call_target="tpu_custom_call" | custom-call | tf_op jit(solution)/shard_map/finish/pallas_call | solution.py:433

commit v4 on v3

--- a/solution.py
+++ b/solution.py
@@ -88,9 +88,9 @@
 
 
 def kernel(
-    gate, up, w, og, lout, ggrad, ugrad, dgrad,
-    gv, uv, wv, hall, ogall, ogc, ogct, part, crecv, ysum, yhalf, yblk, hsend, hrecv, lov,
-    gelu_s, us_s, ggv, guv, acc, losend, lorecv, own, gdv, sems,
+    gate, up, w, og, lov, ggv, guv, gdv,
+    gv, uv, wv, hall, ogall, ogc, ogct, part, crecv, ysum, yhalf, yblk, hsend, hrecv,
+    gelu_s, us_s, acc, losend, lorecv, own, sems,
 ):
     idx = {a: lax.axis_index(a) for a in AXES}
     z, lo, y, hi, c = (idx[a] for a in AXES)
@@ -260,7 +260,6 @@
         remote(ysum.at[shifted("y", 3)], yblk.at[1], "y", 3),
     ]
     hi_send = remote(hsend, hrecv, "hi", 1)
-    store_lout = local(lov, lout)
 
     def scatter_far():
         ysum[y2] = (part[y2, :, c].astype(F32) + crecv[y2].astype(F32)).astype(BF)
@@ -282,7 +281,6 @@
 
     def scatter_end():
         lov[...] = (mine(hi) + hrecv[...].astype(F32)).astype(BF)
-        store_lout.start()
 
     add("scatter core", 3, starts=core_send.values(), after=[("forward", j) for j in tiles])
     add("scatter far", 3, scatter_far, (core_send[2],), half_send, cost=0.3)
@@ -292,8 +290,6 @@
     add("scatter hi", 3, scatter_hi, (core_send[0], *blk_send), (hi_send,), cost=0.2)
     add("scatter end", 3, scatter_end, (hi_send,), cost=0.2)
 
-    stores = []
-
     def backward(k):
         cols = chunk_cols(k)
         group = ogall[...].reshape(TOK, D)
@@ -302,10 +298,6 @@
         )
         ggv[:, cols] = (grad * us_s[:, cols]).astype(BF)
         guv[:, cols] = (grad * gelu_s[:, cols]).astype(BF)
-        for src, dst in ((ggv, ggrad), (guv, ugrad)):
-            copy = local(src.at[:, cols], dst.at[:, cols])
-            copy.start()
-            stores.append(copy)
 
     for k in chunks:
         add(("backward", k), 6, lambda k=k: backward(k), after=[("rows", 8)], cost=1.1 * WIDTHS[k] / 256)
@@ -342,9 +334,6 @@
     def weight_end(k):
         cols = chunk_cols(k)
         gdv[:, cols] = (own[:, cols] + lorecv[:, cols].astype(F32)).astype(BF)
-        copy = local(gdv.at[:, cols], dgrad.at[:, cols])
-        copy.start()
-        stores.append(copy)
 
     transposed = [("transpose", s) for s in range(8)]
     for k in chunks:
@@ -358,39 +347,31 @@
         add(("end", k), 3, lambda k=k: weight_end(k), (lo_send[k],), cost=0.2 * size)
 
     steps.emit()
-    store_lout.wait()
-    for copy in stores:
-        copy.wait()
 
 
 def body(gate, up, w, og):
     any_spec = pl.BlockSpec(memory_space=pl.ANY)
-    shapes = (
-        jax.ShapeDtypeStruct((ROWS, D), BF),
-        jax.ShapeDtypeStruct((TOK, HB), BF),
-        jax.ShapeDtypeStruct((TOK, HB), BF),
-        jax.ShapeDtypeStruct((OUT_COLS, HB), BF),
-    )
     v = pltpu.VMEM
+    shapes = (v((ROWS, D), BF), v((TOK, HB), BF), v((TOK, HB), BF), v((OUT_COLS, HB), BF))
     scratch = [
         v((TOK, HB), BF), v((TOK, HB), BF), v((HB, D), BF),
         v((8 * TOK, HB), BF), v((4, 2, 2, ROWS, D), BF), v((4, 2, 2, 8, ROWS, COLS), BF),
         v((COLS, 8 * TOK), BF),
         v((4, 2, 2, ROWS, D), BF), v((4, 2, ROWS, D), BF), v((4, 2, ROWS, D), BF),
-        v((2, ROWS, D), BF), v((2, 2, ROWS, D), BF), v((ROWS, D), BF), v((ROWS, D), BF), v((ROWS, D), BF),
-        v((TOK, HB), F32), v((TOK, HB), F32), v((TOK, HB), BF), v((TOK, HB), BF),
+        v((2, ROWS, D), BF), v((2, 2, ROWS, D), BF), v((ROWS, D), BF), v((ROWS, D), BF),
+        v((TOK, HB), F32), v((TOK, HB), F32),
         v((2 * OUT_COLS, HB), F32),
-        v((OUT_COLS, HB), BF), v((OUT_COLS, HB), BF), v((OUT_COLS, HB), F32), v((OUT_COLS, HB), BF),
+        v((OUT_COLS, HB), BF), v((OUT_COLS, HB), BF), v((OUT_COLS, HB), F32),
         pltpu.SemaphoreType.DMA((256,)),
     ]
     results = pl.pallas_call(
         kernel,
         out_shape=shapes,
         in_specs=[any_spec] * 4,
-        out_specs=(any_spec,) * 4,
+        out_specs=(pl.BlockSpec(memory_space=pltpu.VMEM),) * 4,
         scratch_shapes=scratch,
         compiler_params=pltpu.CompilerParams(
-            collective_id=0, has_side_effects=True, vmem_limit_bytes=60 * 2**20
+            collective_id=0, has_side_effects=True, vmem_limit_bytes=54 * 2**20
         ),
         cost_estimate=pl.CostEstimate(
             flops=6 * TOK * HB * D, bytes_accessed=14_000_000, transcendentals=TOK * HB
@@ -402,42 +383,30 @@
 
 
 def finish_kernel(*refs):
-    n = len(refs) // 3
-    sources, targets, held = refs[:n], refs[n : 2 * n], refs[2 * n : 3 * n]
-    sems = refs[3 * n]
-    moves = []
-    for source, target, mid in zip(sources, targets, held):
+    n = len(refs) // 2
+    copies = []
+    for source, target in zip(refs[:n], refs[n : 2 * n]):
         rows = source.shape[0]
         pieces = 1 if rows < 128 else 4 if rows % 64 == 0 else 3
         for piece in range(pieces):
             part = pl.ds(piece * (rows // pieces), rows // pieces)
-            k = len(moves)
-            moves.append(
-                (
-                    pltpu.make_async_copy(source.at[part], mid.at[part], sems.at[0, k]),
-                    pltpu.make_async_copy(mid.at[part], target.at[part], sems.at[1, k]),
-                )
-            )
-    for first, _ in moves:
-        first.start()
-    for first, second in moves:
-        first.wait()
-        second.start()
-    for _, second in moves:
-        second.wait()
+            sem = refs[2 * n].at[len(copies)]
+            copies.append(pltpu.make_async_copy(source.at[part], target.at[part], sem))
+    for copy in copies:
+        copy.start()
+    for copy in copies:
+        copy.wait()
 
 
 def finish(results):
-    any_spec = pl.BlockSpec(memory_space=pl.ANY)
     n = len(results)
     return pl.pallas_call(
         finish_kernel,
         out_shape=tuple(jax.ShapeDtypeStruct(r.shape, r.dtype) for r in results),
-        in_specs=[any_spec] * n,
-        out_specs=(any_spec,) * n,
-        scratch_shapes=[pltpu.VMEM(r.shape, r.dtype) for r in results]
-        + [pltpu.SemaphoreType.DMA((2, 4 * n))],
-        compiler_params=pltpu.CompilerParams(vmem_limit_bytes=60 * 2**20),
+        in_specs=[pl.BlockSpec(memory_space=pltpu.VMEM)] * n,
+        out_specs=(pl.BlockSpec(memory_space=pl.ANY),) * n,
+        scratch_shapes=[pltpu.SemaphoreType.DMA((4 * n,))],
+        compiler_params=pltpu.CompilerParams(vmem_limit_bytes=16 * 2**20),
         name="finish",
     )(*results)
 

time: 70.7 us -> 69 us (0.976)
  Pallas kernels: 69.8 us -> 68.2 us
    pallas_call x1, Pallas kernels: 2.57 us -> 1.41 us  [finish(): pl.pallas_call(finish_kernel, out_shape=tuple((jax.ShapeDtypeStruct(r.sha...]
where the time goes in v4:
time: 69 us; the launch traced here: 68.8 us
  Pallas kernels  68.2 us (99%)
    pallas_call x1, Pallas kernels, body(): pl.pallas_call(kernel, out_shape=shapes, in_specs=[any_spec] * 4, out_spe...  66.8 us
    pallas_call x1, Pallas kernels, finish(): pl.pallas_call(finish_kernel, out_shape=tuple((jax.ShapeDtypeStruct(r.sha...  1.41 us

profile of v4, /device:TPU:16, one launch (start us, length us, event | category | flops | bytes accessed | tf_op | source)
XLA Modules:
  0.0 68.8 jit_solution(3926498017039044124)
XLA Ops:
  0.6 66.8 %geglu_down.1 = (bf16[16,4608]{1,0:T(8,128)(2,1)S(1)}, bf16[256,1152]{1,0:T(8,128)(2,1)S(1)}, bf16[256,1152]{1,0:T(8,128)(2,1)S(1)}, bf16[288,1152]{1,0:T(8,128)(2,1)S(1)}) custom-call(bf16[256,1152]{1,0:T(8,128)(2,1)} %gate.1, bf16[256,1152]{1,0:T(8,128)(2,1)} %up.1, bf16[1152,4608]{1,0:T(8,128)(2,1)} %w.1, bf16[16,4608]{1,0:T(8,128)(2,1)} %og.1), custom_call_target="tpu_custom_call" | custom-call | flops 8153726976 | bytes 14000000 | tf_op jit(solution)/shard_map/geglu_down/pallas_call | solution.py:367
  67.4 1.4 %finish.1 = (bf16[16,4608]{1,0:T(8,128)(2,1)}, bf16[256,1152]{1,0:T(8,128)(2,1)}, bf16[256,1152]{1,0:T(8,128)(2,1)}, bf16[288,1152]{1,0:T(8,128)(2,1)}) custom-call(bf16[16,4608]{1,0:T(8,128)(2,1)S(1)} %get-tuple-element.12.refs_0_, bf16[256,1152]{1,0:T(8,128)(2,1)S(1)} %get-tuple-element.13.refs_1_, bf16[256,1152]{1,0:T(8,128)(2,1)S(1)} %get-tuple-element.14.refs_2_, ...), custom_call_target="tpu_custom_call" | custom-call | tf_op jit(solution)/shard_map/finish/pallas_call | solution.py:403

commit v5 on v4

--- a/solution.py
+++ b/solution.py
@@ -31,7 +31,7 @@
     return gelu, slope
 
 
-LANES = dict(z=(20.2, 2.0), y=(20.2, 2.6), x=(20.2, 2.6), core=(4.0, 2.0))
+LANES = dict(z=(19.4, 1.8), y=(20.2, 2.6), x=(20.2, 2.6), core=(4.0, 2.0))
 
 
 class Move:
@@ -148,14 +148,15 @@
     load_w = [
         local(w.at[:, pl.ds(j * WT, WT)], wv.at[:, pl.ds(j * WT, WT)]) for j in range(D // WT)
     ]
-    for pair in loads[:1]:
-        pair[0].start()
-        pair[1].start()
+    order = [k for k, hop in Z_ORDER if hop == 0]
+    for k in order[:1]:
+        loads[k][0].start()
+        loads[k][1].start()
     load_og.start()
     load_ogc.start()
-    for pair in loads[1:]:
-        pair[0].start()
-        pair[1].start()
+    for k in order[1:]:
+        loads[k][0].start()
+        loads[k][1].start()
     for copy in load_w:
         copy.start()
 
@@ -175,7 +176,8 @@
     pl.semaphore_wait(barrier, len(peers))
 
     a2a = [
-        remote(og.at[:, window(shifted("z", d))], ogc.at[y, hi, c, d], "z", d) for d in range(1, 8)
+        remote(og.at[:, window(shifted("z", d))], ogc.at[y, hi, c, d], "z", d)
+        for d in (4, 3, 5, 2, 6, 1, 7)
     ]
     add("columns out", 0, starts=a2a)
 
@@ -230,10 +232,10 @@
                 after.append(("hidden", k))
             waits = (hops[k, hop - 1, way],) if hop else ()
             add(("z", k, hop, way), 1, waits=waits, starts=(hops[k, hop, way],), after=after)
-    for k in chunks:
+    for i, k in enumerate(order):
         add(
-            ("hidden", k), 0 if k < 2 else 4, lambda k=k: hidden(k), cost=0.9 * WIDTHS[k] / 256,
-            after=[("hidden", k - 1) if k else "columns out"],
+            ("hidden", k), 0 if i < 3 else 4, lambda k=k: hidden(k), cost=0.9 * WIDTHS[k] / 256,
+            after=[("hidden", order[i - 1]) if i else "columns out"],
         )
 
     def forward(j):

time: 69 us -> 68.9 us (level)
  no operation moved by 1% of the time
where the time goes in v5:
time: 68.9 us
  Pallas kernels  68.2 us (99%)
    pallas_call x1, Pallas kernels, body(): pl.pallas_call(kernel, out_shape=shapes, in_specs=[any_spec] * 4, out_spe...  66.8 us
    pallas_call x1, Pallas kernels, finish(): pl.pallas_call(finish_kernel, out_shape=tuple((jax.ShapeDtypeStruct(r.sha...  1.41 us

profile of v5, /device:TPU:16, one launch (start us, length us, event | category | flops | bytes accessed | tf_op | source)
XLA Modules:
  0.0 68.9 jit_solution(17190076612184278914)
XLA Ops:
  0.6 66.8 %geglu_down.1 = (bf16[16,4608]{1,0:T(8,128)(2,1)S(1)}, bf16[256,1152]{1,0:T(8,128)(2,1)S(1)}, bf16[256,1152]{1,0:T(8,128)(2,1)S(1)}, bf16[288,1152]{1,0:T(8,128)(2,1)S(1)}) custom-call(bf16[256,1152]{1,0:T(8,128)(2,1)} %gate.1, bf16[256,1152]{1,0:T(8,128)(2,1)} %up.1, bf16[1152,4608]{1,0:T(8,128)(2,1)} %w.1, bf16[16,4608]{1,0:T(8,128)(2,1)} %og.1), custom_call_target="tpu_custom_call" | custom-call | flops 8153726976 | bytes 14000000 | tf_op jit(solution)/shard_map/geglu_down/pallas_call | solution.py:369
  67.4 1.4 %finish.1 = (bf16[16,4608]{1,0:T(8,128)(2,1)}, bf16[256,1152]{1,0:T(8,128)(2,1)}, bf16[256,1152]{1,0:T(8,128)(2,1)}, bf16[288,1152]{1,0:T(8,128)(2,1)}) custom-call(bf16[16,4608]{1,0:T(8,128)(2,1)S(1)} %get-tuple-element.12.refs_0_, bf16[256,1152]{1,0:T(8,128)(2,1)S(1)} %get-tuple-element.13.refs_1_, bf16[256,1152]{1,0:T(8,128)(2,1)S(1)} %get-tuple-element.14.refs_2_, ...), custom_call_target="tpu_custom_call" | custom-call | tf_op jit(solution)/shard_map/finish/pallas_call | solution.py:405
